TPU v7x, 128 devices: a whole 4x4x4 slice. The times are simulated.
128 devices in a mesh: emit: 8 (over x_hi, z), elem: 16 (over y, x_lo, core).
Axes of the slice: x: 4 (x_hi: 2, x_lo: 2; x = x_hi * 2 + x_lo), y: 4, z: 4, core: 2. Of those that a mesh axis runs over, the one named last changes fastest.
Arguments:
- traces: float32 [256, 1024, 1024], P('emit', 'elem'), may hold values from -6 to 6
- codes: float32 [4, 2, 128], replicated, may hold values from -0.5 to 0.5
- code_of: int32 [256], replicated, may hold values from 0 to 3
- order: int32 [256], replicated, may hold values from 0 to 255, each once
- steer: float32 [256, 1024, 256], P(None, 'elem'), may hold values from -0.1875 to 0.1875
Outputs:
- beams: float32 [256, 256, 256], P('elem', 'emit')
Inputs may be any that keep to these rules, and one draw needn't show every extreme that they name: `order`: each value 0 to 255 appears exactly once.
All inputs are finite; a program needn't handle non-finite values.
Results may differ from a plain program's by a relative error of at most 0.000071.
Values sent between devices are 32-bit elements; how exact they have to be, the bound alone decides.
A program may use at most 192 MiB of HBM per device.

v0:
```python
import jax
import jax.numpy as jnp
from jax import lax
from jax.sharding import PartitionSpec as P


def toeplitz_table(codes):
    taps = codes.shape[2]
    rows = jnp.arange(2 * taps, dtype=jnp.int32)[:, None]
    cols = jnp.arange(taps, dtype=jnp.int32)[None, :]
    offset = rows - cols
    inside = (offset >= 0) & (offset < taps)
    clipped = jnp.clip(offset, 0, taps - 1)
    in_phase = jnp.where(inside[None], codes[:, 0, :][:, clipped], 0.0)
    quadrature = jnp.where(inside[None], codes[:, 1, :][:, clipped], 0.0)
    return jnp.concatenate([in_phase, quadrature], axis=2)


def hadamard_signs(order, columns, emissions):
    parity = jnp.zeros((order.shape[0], columns.shape[0]), jnp.int32)
    for bit in range(emissions.bit_length()):
        parity = parity + (order[:, None] >> bit & columns[None, :] >> bit & 1)
    signs = (1 - 2 * (parity % 2)).astype(jnp.float32)
    return signs / jnp.sqrt(jnp.float32(emissions))


def spectral_table(samples, taps, bins):
    rows = jnp.arange(samples // taps * 2 * taps, dtype=jnp.int32)
    block = rows // (2 * taps)
    quad = rows // taps % 2
    sample = block * taps + rows % taps
    freqs = jnp.arange(bins, dtype=jnp.int32) - bins // 2
    phase = jnp.mod(sample[:, None] * freqs[None, :], samples).astype(jnp.float32)
    angle = phase * (2.0 * jnp.pi / samples)
    cosine = jnp.cos(angle)
    sine = jnp.sin(angle)
    is_quad = quad[:, None] == 1
    real_cols = jnp.where(is_quad, sine, cosine)
    imag_cols = jnp.where(is_quad, cosine, -sine)
    return jnp.concatenate([real_cols, imag_cols], axis=1) / jnp.sqrt(jnp.float32(samples))


def steer_bins(source, steer, count, contract):
    bins = steer.shape[0]
    half = steer.shape[2] // 2
    real_part = lax.slice_in_dim(source, 0, count, axis=0)
    imag_part = lax.dynamic_slice_in_dim(source, bins, count, 0)
    numbers = (((contract,), (1,)), ((0,), (0,)))
    first = lax.dot_general(real_part, steer, numbers, precision=lax.Precision.HIGHEST)
    second = lax.dot_general(imag_part, steer, numbers, precision=lax.Precision.HIGHEST)
    return jnp.concatenate(
        [first[..., :half] - second[..., half:], first[..., half:] + second[..., :half]], axis=2
    )


def per_device(traces, codes, code_of, order, steer):
    edev, mdev, samples = traces.shape
    ncode, taps = (codes.shape[0], codes.shape[2])
    emissions = order.shape[0]
    bins = steer.shape[0]
    bins_dev = bins // lax.axis_size("elem")
    nblock = samples // taps
    first = lax.axis_index("emit") * edev
    own_codes = lax.dynamic_slice_in_dim(code_of, first, edev)
    onehot = (own_codes[:, None] == jnp.arange(ncode, dtype=jnp.int32)[None, :]).astype(jnp.float32)
    table = toeplitz_table(codes)
    picked = jnp.einsum("ec,cjd->ejd", onehot, table, precision=lax.Precision.HIGHEST)
    blocks = traces.reshape(edev, mdev, nblock, taps)
    current = jnp.einsum(
        "emnj,ejd->emnd", blocks, picked[:, :taps, :], precision=lax.Precision.HIGHEST
    )
    following = jnp.einsum(
        "emnj,ejd->emnd", blocks, picked[:, taps:, :], precision=lax.Precision.HIGHEST
    )
    following = jnp.concatenate(
        [following[:, :, 1:], jnp.zeros((edev, mdev, 1, 2 * taps), jnp.float32)], axis=2
    )
    corr = (current + following).reshape(edev, mdev, nblock * 2 * taps)
    transform = spectral_table(samples, taps, bins)
    spectra = lax.dot_general(
        transform, corr, (((0,), (2,)), ((), ())), precision=lax.Precision.HIGHEST
    )
    columns = first + jnp.arange(edev, dtype=jnp.int32)
    hadamard = hadamard_signs(order, columns, emissions)
    decoded = lax.dot_general(
        lax.all_gather(spectra, "emit", axis=1, tiled=True),
        hadamard,
        (((1,), (0,)), ((), ())),
        precision=lax.Precision.HIGHEST,
    )
    return lax.psum_scatter(
        steer_bins(decoded, steer, bins_dev * lax.axis_size("elem"), 1),
        "elem",
        scatter_dimension=0,
        tiled=True,
    )


def solution(mesh):
    placed = (P("emit", "elem", None), P(), P(), P(), P(None, "elem", None))
    return jax.shard_map(
        per_device, mesh=mesh, in_specs=placed, out_specs=P("elem", "emit", None), check_vma=False
    )
```

profile of v0, /device:TPU:0, one launch (start us, length us, event | category | flops | bytes accessed | tf_op | source)
XLA Modules:
  0.0 918.1 jit_solution(17875614214764076729)
XLA Ops:
  6.5 0.0 all-gather.2.cloned.1.call-start
  6.5 0.1 fusion.23
  6.7 0.8 fusion.93
  7.5 0.1 copy.40
  7.6 108.5 %gather_fusion = f32[32768,4]{1,0:T(8,128)} fusion(f32[4,128]{0,1:T(8,128)S(1)} %bitcast.52, s32[32768]{0:T(1024)S(1)} %fusion.23), kind=kCustom, calls=%fused_computation | custom fusion | bytes 1179648 | tf_op jit(solution)/shard_map/gather | solution.py:14
  116.0 9.4 %copy.16 = f32[256,128,4]{1,2,0:T(4,128)S(1)} copy(f32[256,128,4]{2,1,0:T(8,128)} %bitcast.56) | data formatting | bytes 1048576 | tf_op jit(solution)/shard_map/gather | solution.py:14
  125.5 0.1 copy.41
  125.6 108.5 %gather_fusion.1 = f32[32768,4]{1,0:T(8,128)} fusion(f32[4,128]{0,1:T(8,128)S(1)} %bitcast.51, s32[32768]{0:T(1024)S(1)} %fusion.23), kind=kCustom, calls=%fused_computation.1 | custom fusion | bytes 1179648 | tf_op jit(solution)/shard_map/gather | solution.py:15
  234.1 0.0 copy-start.2
  234.1 9.4 %copy.19 = f32[256,128,4]{1,2,0:T(4,128)S(1)} copy(f32[256,128,4]{2,1,0:T(8,128)} %bitcast.55) | data formatting | bytes 1048576 | tf_op jit(solution)/shard_map/gather | solution.py:15
  243.5 0.0 copy-done.2
  243.5 0.1 dynamic_slice.6
  243.6 0.3 select_bitcast_fusion.1
  243.9 0.0 slice-start
  243.9 5.9 fusion.15
  249.8 0.0 slice-start.1
  249.8 6.8 slice_bitcast_fusion.1
  256.6 0.0 slice-done
  256.6 0.0 slice-done.1
  256.6 17.6 %convolution_bitcast_fusion = f32[32,64,8,256]{3,1,2,0:T(8,128)} fusion(f32[32,128,256,1]{2,0,1,3:T(8,128)S(1)} %get-tuple-element.8, f32[32,64,1024]{2,1,0:T(8,128)S(1)} %bitcast.54), kind=kOutput, calls=%fused_computation.3 | convolution fusion | flops 6442450944 | bytes 29360128 | tf_op jit(solution)/shard_map/emnj,ejd->emnd/dot_general | solution.py:72
  274.2 13.1 %slice.46 = f32[32,64,7,256]{3,1,2,0:T(8,128)} slice(f32[32,64,8,256]{3,1,2,0:T(8,128)} %convolution_bitcast_fusion), slice={[0:32], [0:64], [1:8], [0:256]} | slice | bytes 29360128 | tf_op jit(solution)/shard_map/slice | solution.py:76
  287.3 29.1 %bitcast_add_fusion = f32[32,64,8,256]{3,1,2,0:T(8,128)} fusion(f32[32,64,7,256]{3,1,2,0:T(8,128)} %slice.46, f32[32,128,256,1]{2,0,1,3:T(8,128)} %get-tuple-element.7, f32[32,64,1024]{2,1,0:T(8,128)} %param.5), kind=kOutput, calls=%fused_computation.2 | convolution fusion | flops 6446645248 | bytes 44040192 | tf_op jit(solution)/shard_map/emnj,ejd->emnd/dot_general | solution.py:69
  316.4 18.2 %copy.38 = f32[32,64,8,256]{3,2,0,1:T(8,128)} copy(f32[32,64,8,256]{3,1,2,0:T(8,128)} %bitcast_add_fusion) | data formatting | bytes 33554432 | tf_op jit(solution)/shard_map/reshape | solution.py:78
  334.6 18.0 %reshape.181 = f32[32,64,2048]{2,0,1:T(8,128)} reshape(f32[32,64,8,256]{3,2,0,1:T(8,128)} %copy.38) | data formatting | bytes 33554432 | tf_op jit(solution)/shard_map/reshape | solution.py:78
  352.5 8.5 fusion.21
  361.1 30.8 %fusion.5 = f32[512,32,64]{0,1,2:T(8,128)} fusion(f32[32,64,2048]{2,0,1:T(8,128)} %reshape.181, f32[2048,256]{1,0:T(8,128)S(1)} %get-tuple-element.14, f32[2048,256]{1,0:T(8,128)S(1)} %get-tuple-element.13), kind=kOutput, calls=%fused_computation.15 | convolution fusion | flops 25771900928 | bytes 25165824 | tf_op jit(solution)/shard_map/dot_general | solution.py:80
  391.8 0.0 copy-start.1
  391.8 0.0 all-gather.2.cloned.1.call-update
  391.9 0.0 reduce-scatter.2.cloned.1.call-start
  392.0 0.5 copy-done.1
  392.5 336.3 %all-gather.2.cloned.1.call-done = f32[512,256,64]{0,1,2:T(8,128)} async-done(((f32[512,32,64]{0,1,2:T(8,128)}), f32[512,256,64]{0,1,2:T(8,128)}) %all-gather.2.cloned.1.call-update) | async-done | bytes 33554448 | tf_op jit(solution)/shard_map/all_gather | solution.py:86
  728.8 25.7 %fusion.33 = f32[512,64,32]{0,2,1:T(8,128)} fusion(f32[512,256,64]{0,1,2:T(8,128)} %all-gather.2.cloned.1.call-done, s32[32]{0:T(128)S(1)} %get-tuple-element.26, s32[256]{0:T(256)S(1)} %get-tuple-element.24, s32[32]{0:T(128)S(1)} %get-tuple-element.27, s32[256]{0:T(256)S(1)} %get-tuple-element.25, s32[32]{0:T(128)S(1)} %get-tuple-element.28, ...), kind=kOutput, calls=%fused_computation.55 | convolution fusion | flops 3221561344 | bytes 37759104 | tf_op jit(solution)/shard_map/dot_general | solution.py:85
  754.6 4.0 fusion.92
  758.6 5.6 copy.25
  764.2 4.5 copy.26
  768.6 0.0 copy-start
  768.7 16.0 %fusion.94 = f32[256,32,256]{2,1,0:T(8,128)} fusion(f32[256,64,32]{1,2,0:T(8,128)} %copy.25, f32[256,64,256]{2,1,0:T(8,128)} %param.9), kind=kOutput, calls=%fused_computation.136 | convolution fusion | flops 1610612736 | bytes 27262976 | tf_op jit(solution)/shard_map/dot_general | solution.py:49
  784.7 0.0 copy-done
  784.7 14.1 %fusion.95 = f32[256,32,256]{2,1,0:T(8,128)} fusion(f32[256,64,32]{1,2,0:T(8,128)S(1)} %copy-done, f32[256,64,256]{2,1,0:T(8,128)} %param.9), kind=kOutput, calls=%fused_computation.137 | convolution fusion | flops 1610612736 | bytes 27262976 | tf_op jit(solution)/shard_map/dot_general | solution.py:50
  798.8 9.9 %slice_subtract_fusion = (f32[256,32,128]{2,1,0:T(8,128)S(1)}, f32[256,32,128]{2,1,0:T(8,128)}) fusion(f32[256,32,256]{2,1,0:T(8,128)} %fusion.95, f32[256,32,256]{2,1,0:T(8,128)} %fusion.94), kind=kLoop, calls=%fused_computation.10 | loop fusion | flops 2097152 | bytes 25165824 | tf_op jit(solution)/shard_map/sub | solution.py:52
  808.7 6.4 pad_maximum_fusion
  815.1 0.0 reduce-scatter.2.cloned.1.call-update
  815.1 95.7 %reduce-scatter.2.cloned.1.call-done = f32[16,32,256]{2,1,0:T(8,128)} async-done(((f32[256,32,256]{2,1,0:T(8,128)}), f32[16,32,256]{2,1,0:T(8,128)}) %reduce-scatter.2.cloned.1.call-update) | async-done | bytes 524304 | tf_op jit(solution)/shard_map/reduce_scatter | solution.py:91
  (11 shorter events, 0.1 us)
Async XLA Ops:
  6.5 722.3 %all-gather.2.cloned.1.call-start = ((), (), s32[]{:S(2)}) async-start(), calls=%async_computation.1 | async-start | bytes 37748736 | tf_op jit(solution)/shard_map/all_gather | solution.py:86
  234.1 9.4 %copy-start.2 = (s32[256]{0:T(256)S(1)}, s32[256]{0:T(256)}, u32[]{:S(2)}) copy-start(s32[256]{0:T(256)} %param.7) | copy-start | bytes 3076
  243.9 12.7 %slice-start = ((s8[8388608]{0:T(1024)(128)(4,1)}), s8[4194304]{0:T(1024)(128)(4,1)S(1)}, s32[]{:S(2)}) async-start(s8[8388608]{0:T(1024)(128)(4,1)} %bitcast.53), calls=%async_computation.3 | async-start | bytes 8388608
  249.8 6.8 slice-start.1
  391.8 0.7 copy-start.1
  391.9 518.9 %reduce-scatter.2.cloned.1.call-start = ((), (), s32[]{:S(2)}) async-start(), calls=%async_computation.2 | async-start | bytes 8912896 | tf_op jit(solution)/shard_map/reduce_scatter | solution.py:91
  768.6 16.0 %copy-start = (f32[256,64,32]{1,2,0:T(8,128)S(1)}, f32[256,64,32]{1,2,0:T(8,128)}, u32[]{:S(2)}) copy-start(f32[256,64,32]{1,2,0:T(8,128)} %copy.26) | copy-start | bytes 6291460
Sparse Core Ops, SparseCore 0:
  392.0 336.7 all-gather.1
  815.2 95.5 reduce-scatter.1
where the time goes:
time: 926 us; the launch traced here: 918 us
  waiting for transfers between devices  432 us (47%)
  local copies, waits for them, and re-layouts  308 us (33%)
  matrix products  139 us (15%)
  other arithmetic  25.2 us (3%)
  between operations  14 us (2%)
    all_gather x1, waiting for transfers between devices, per_device(): lax.all_gather(spectra, 'emit', axis=1, tiled=True)  336 us
    gather x2, local copies, waits for them, and re-layouts, toeplitz_table(): quadrature = jnp.where(inside[None], codes[:, 1, :][:, clipped], 0.0)  118 us
    gather x2, local copies, waits for them, and re-layouts, toeplitz_table(): in_phase = jnp.where(inside[None], codes[:, 0, :][:, clipped], 0.0)  118 us
    reduce_scatter x1, waiting for transfers between devices, per_device(): lax.psum_scatter(steer_bins(decoded, steer, bins_dev * lax.axis_size('ele...  95.7 us
    reshape x2, local copies, waits for them, and re-layouts, per_device(): corr = (current + following).reshape(edev, mdev, nblock * 2 * taps)  36.1 us
    dot_general x1, matrix products, per_device(): lax.dot_general(transform, corr, (((0,), (2,)), ((), ())), precision=lax....  30.8 us
    dot_general x1, matrix products, per_device(): jnp.einsum('emnj,ejd->emnd', blocks, picked[:, :taps, :], precision=lax.P...  29.1 us
    dot_general x1, matrix products, per_device(): lax.dot_general(lax.all_gather(spectra, 'emit', axis=1, tiled=True), hada...  25.7 us
  transfers between devices with their start and end apart: 2, of which 2 were waited for; matrix products, arithmetic and copies ran while one was open for 0% of the time, Pallas kernels for 0%

commit v1 on v0

--- a/solution.py
+++ b/solution.py
@@ -2,6 +2,11 @@
 import jax.numpy as jnp
 from jax import lax
 from jax.sharding import PartitionSpec as P
+
+
+def gather_over(x, axis, along):
+    sent = jnp.stack([x] * lax.axis_size(axis))
+    return jnp.concatenate(lax.all_to_all(sent, axis, 0, 0), axis=along)
 
 
 def toeplitz_table(codes):
@@ -83,7 +88,7 @@
     columns = first + jnp.arange(edev, dtype=jnp.int32)
     hadamard = hadamard_signs(order, columns, emissions)
     decoded = lax.dot_general(
-        lax.all_gather(spectra, "emit", axis=1, tiled=True),
+        gather_over(spectra, "emit", 1),
         hadamard,
         (((1,), (0,)), ((), ())),
         precision=lax.Precision.HIGHEST,

time: 926 us -> 963 us (1.040)
  waiting for transfers between devices: 432 us -> 461 us
  matrix products: 139 us -> 156 us
  local copies, waits for them, and re-layouts: 308 us -> 291 us
    all_to_all x0 -> x1, waiting for transfers between devices: none -> 364 us  [gather_over(): return jnp.concatenate(lax.all_to_all(sent, axis, 0, 0), axis=along)]
    all_gather x1 -> x0, waiting for transfers between devices: 336 us -> none  [per_device(): lax.all_gather(spectra, 'emit', axis=1, tiled=True)]
    reshape x2 -> x1, local copies, waits for them, and re-layouts: 36.1 us -> 7.58 us  [per_device(): corr = (current + following).reshape(edev, mdev, nblock * 2 * taps)]
    dot_general x1, matrix products: 25.7 us -> 45.2 us  [per_device(): lax.dot_general(gather_over(spectra, 'emit', 1), hadamard, (((1,), (0,)),...]
    another operation x0 -> x1, local copies, waits for them, and re-layouts: none -> 11.4 us  [gather_over(): sent = jnp.stack([x] * lax.axis_size(axis))]
where the time goes in v1:
time: 963 us; the launch traced here: 956 us
  waiting for transfers between devices  461 us (48%)
  local copies, waits for them, and re-layouts  291 us (30%)
  matrix products  156 us (16%)
  other arithmetic  25.2 us (3%)
  between operations  14.1 us (1%)
    all_to_all x1, waiting for transfers between devices, gather_over(): return jnp.concatenate(lax.all_to_all(sent, axis, 0, 0), axis=along)  364 us
    gather x2, local copies, waits for them, and re-layouts, toeplitz_table(): quadrature = jnp.where(inside[None], codes[:, 1, :][:, clipped], 0.0)  118 us
    gather x2, local copies, waits for them, and re-layouts, toeplitz_table(): in_phase = jnp.where(inside[None], codes[:, 0, :][:, clipped], 0.0)  118 us
    reduce_scatter x1, waiting for transfers between devices, per_device(): lax.psum_scatter(steer_bins(decoded, steer, bins_dev * lax.axis_size('ele...  97.5 us
    dot_general x1, matrix products, per_device(): lax.dot_general(gather_over(spectra, 'emit', 1), hadamard, (((1,), (0,)),...  45.2 us
    dot_general x1, matrix products, per_device(): jnp.einsum('emnj,ejd->emnd', blocks, picked[:, :taps, :], precision=lax.P...  29.2 us
    dot_general x1, matrix products, per_device(): lax.dot_general(transform, corr, (((0,), (2,)), ((), ())), precision=lax....  28.1 us
  transfers between devices with their start and end apart: 2, of which 2 were waited for; matrix products, arithmetic and copies ran while one was open for 0% of the time, Pallas kernels for 0%

profile of v1, /device:TPU:0, one launch (start us, length us, event | category | flops | bytes accessed | tf_op | source)
XLA Modules:
  0.0 955.7 jit_solution(10511183601115813765)
XLA Ops:
  6.5 0.1 fusion.26
  6.7 0.8 fusion.95
  7.4 0.1 copy.39
  7.6 109.0 %gather_fusion = f32[32768,4]{1,0:T(8,128)} fusion(f32[4,128]{0,1:T(8,128)S(1)} %bitcast.55, s32[32768]{0:T(1024)S(1)} %fusion.26), kind=kCustom, calls=%fused_computation | custom fusion | bytes 1179648 | tf_op jit(solution)/shard_map/gather | solution.py:19
  116.6 9.4 copy.17
  126.0 0.1 copy.40
  126.1 109.0 %gather_fusion.1 = f32[32768,4]{1,0:T(8,128)} fusion(f32[4,128]{0,1:T(8,128)S(1)} %bitcast.54, s32[32768]{0:T(1024)S(1)} %fusion.26), kind=kCustom, calls=%fused_computation.1 | custom fusion | bytes 1179648 | tf_op jit(solution)/shard_map/gather | solution.py:20
  235.1 0.0 copy-start.2
  235.1 9.4 copy.20
  244.5 0.0 copy-done.2
  244.5 0.1 dynamic_slice.6
  244.6 0.3 select_bitcast_fusion.1
  244.9 0.0 slice-start
  244.9 5.9 fusion.18
  250.8 0.0 slice-start.1
  250.8 6.8 slice_bitcast_fusion.1
  257.6 0.0 slice-done
  257.6 0.0 slice-done.1
  257.6 17.7 %convolution_bitcast_fusion = f32[32,64,8,256]{3,1,2,0:T(8,128)} fusion(f32[32,128,256,1]{2,0,1,3:T(8,128)S(1)} %get-tuple-element.8, f32[32,64,1024]{2,1,0:T(8,128)S(1)} %bitcast.57), kind=kOutput, calls=%fused_computation.6 | convolution fusion | flops 6442450944 | bytes 29360128 | tf_op jit(solution)/shard_map/emnj,ejd->emnd/dot_general | solution.py:77
  275.3 13.1 %slice.46 = f32[32,64,7,256]{3,1,2,0:T(8,128)} slice(f32[32,64,8,256]{3,1,2,0:T(8,128)} %convolution_bitcast_fusion), slice={[0:32], [0:64], [1:8], [0:256]} | slice | bytes 29360128 | tf_op jit(solution)/shard_map/slice | solution.py:81
  288.4 29.2 %fusion.2 = f32[32,8,8,8,256]{4,3,2,1,0:T(8,128)} fusion(f32[32,64,7,256]{3,1,2,0:T(8,128)} %slice.46, f32[32,128,256,1]{2,0,1,3:T(8,128)} %get-tuple-element.7, f32[32,64,1024]{2,1,0:T(8,128)} %param.5), kind=kOutput, calls=%fused_computation.5 | convolution fusion | flops 6446645248 | bytes 44040192 | tf_op jit(solution)/shard_map/emnj,ejd->emnd/dot_general | solution.py:74
  317.6 7.6 copy.42
  325.2 8.5 fusion.24
  333.7 28.1 %fusion.8 = f32[512,32,64]{0,2,1:T(8,128)S(1)} fusion(f32[32,64,2048]{2,1,0:T(8,128)S(1)} %bitcast.60, f32[2048,256]{1,0:T(8,128)S(1)} %get-tuple-element.14, f32[2048,256]{1,0:T(8,128)S(1)} %get-tuple-element.13), kind=kOutput, calls=%fused_computation.18 | convolution fusion | flops 25771900928 | bytes 25165824 | tf_op jit(solution)/shard_map/dot_general | solution.py:85
  361.8 11.4 %stack.2 = f32[8,512,32,64]{1,3,2,0:T(8,128)} broadcast(f32[512,32,64]{0,2,1:T(8,128)S(1)} %fusion.8), dimensions={1,2,3} | broadcast | bytes 37748736 | tf_op jit(solution)/shard_map/stack | solution.py:8
  373.2 0.0 copy-start.1
  373.2 8.0 all-to-all-start
  381.2 0.0 reduce-scatter.2.cloned.1.call-start
  381.3 0.0 copy-done.1
  381.3 363.5 %all-to-all-done = f32[8,512,32,64]{1,3,2,0:T(8,128)} async-done(((f32[8,512,32,64]{1,3,2,0:T(8,128)}), f32[8,512,32,64]{1,3,2,0:T(8,128)}, u32[]{:S(2)}, u32[]{:S(2)}) %all-to-all-start) | async-done | bytes 33554464 | tf_op jit(solution)/shard_map/all_to_all | solution.py:9
  744.8 45.2 %fusion = f32[512,64,32]{0,2,1:T(8,128)} fusion(f32[512,256,64]{0,2,1:T(8,128)} %bitcast.14, s32[32]{0:T(128)S(1)} %get-tuple-element.26, s32[256]{0:T(256)S(1)} %get-tuple-element.24, s32[32]{0:T(128)S(1)} %get-tuple-element.27, s32[256]{0:T(256)S(1)} %get-tuple-element.25, s32[32]{0:T(128)S(1)} %get-tuple-element.28, s32[256]{0:T(256)S(1)} %get-tuple-element.18, ...), kind=kOutput, calls=%fused_computation.2 | convolution fusion | flops 3221561344 | bytes 37759104 | tf_op jit(solution)/shard_map/dot_general | solution.py:90
  790.0 4.0 fusion.94
  794.0 5.6 copy.27
  799.6 4.7 copy.28
  804.3 0.0 copy-start
  804.3 15.8 %fusion.96 = f32[256,32,256]{2,1,0:T(8,128)} fusion(f32[256,64,32]{1,2,0:T(8,128)} %copy.27, f32[256,64,256]{2,1,0:T(8,128)} %param.9), kind=kOutput, calls=%fused_computation.138 | convolution fusion | flops 1610612736 | bytes 27262976 | tf_op jit(solution)/shard_map/dot_general | solution.py:54
  820.1 0.0 copy-done
  820.1 14.3 %fusion.97 = f32[256,32,256]{2,1,0:T(8,128)} fusion(f32[256,64,32]{1,2,0:T(8,128)S(1)} %copy-done, f32[256,64,256]{2,1,0:T(8,128)} %param.9), kind=kOutput, calls=%fused_computation.139 | convolution fusion | flops 1610612736 | bytes 27262976 | tf_op jit(solution)/shard_map/dot_general | solution.py:55
  834.5 9.9 %slice_subtract_fusion = (f32[256,32,128]{2,1,0:T(8,128)S(1)}, f32[256,32,128]{2,1,0:T(8,128)}) fusion(f32[256,32,256]{2,1,0:T(8,128)} %fusion.97, f32[256,32,256]{2,1,0:T(8,128)} %fusion.96), kind=kLoop, calls=%fused_computation.13 | loop fusion | flops 2097152 | bytes 25165824 | tf_op jit(solution)/shard_map/sub | solution.py:57
  844.4 6.4 pad_maximum_fusion
  850.7 0.0 reduce-scatter.2.cloned.1.call-update
  850.8 97.5 %reduce-scatter.2.cloned.1.call-done = f32[16,32,256]{2,1,0:T(8,128)} async-done(((f32[256,32,256]{2,1,0:T(8,128)}), f32[16,32,256]{2,1,0:T(8,128)}) %reduce-scatter.2.cloned.1.call-update) | async-done | bytes 524304 | tf_op jit(solution)/shard_map/reduce_scatter | solution.py:96
  (11 shorter events, 0.1 us)
Async XLA Ops:
  235.1 9.4 copy-start.2
  244.9 12.7 %slice-start = ((s8[8388608]{0:T(1024)(128)(4,1)}), s8[4194304]{0:T(1024)(128)(4,1)S(1)}, s32[]{:S(2)}) async-start(s8[8388608]{0:T(1024)(128)(4,1)} %bitcast.56), calls=%async_computation.3 | async-start | bytes 8388608
  250.8 6.8 slice-start.1
  373.2 8.1 copy-start.1
  373.2 371.6 %all-to-all-start = ((f32[8,512,32,64]{1,3,2,0:T(8,128)}), f32[8,512,32,64]{1,3,2,0:T(8,128)}, u32[]{:S(2)}, u32[]{:S(2)}) async-start(f32[8,512,32,64]{1,3,2,0:T(8,128)} %stack.2), calls=%async_computation | async-start | bytes 67108864 | tf_op jit(solution)/shard_map/all_to_all | solution.py:9
  381.2 567.1 %reduce-scatter.2.cloned.1.call-start = ((), (), s32[]{:S(2)}) async-start(), calls=%async_computation.2 | async-start | bytes 8912896 | tf_op jit(solution)/shard_map/reduce_scatter | solution.py:96
  804.3 15.8 %copy-start = (f32[256,64,32]{1,2,0:T(8,128)S(1)}, f32[256,64,32]{1,2,0:T(8,128)}, u32[]{:S(2)}) copy-start(f32[256,64,32]{1,2,0:T(8,128)} %copy.28) | copy-start | bytes 6291460
Sparse Core Ops, SparseCore 0:
  850.9 97.3 reduce-scatter.1
